TPU v7x, 256 devices: a whole 4x4x8 slice. The times are simulated.
256 devices in a mesh: seq: 128 (over x, z, y), rows: 2 (over core).
Axes of the slice: x: 4, y: 4, z: 8, core: 2. Of those that a mesh axis runs over, the one named last changes fastest.
Arguments:
- queries: bfloat16 [2, 8, 8192], P(None, None, 'seq'), may hold values from -6 to 6
- new_keys: bfloat16 [2, 8, 1024], P(None, None, 'seq'), may hold values from -16 to 16
- new_values: bfloat16 [2, 8, 1024], P(None, None, 'seq'), may hold values from -6 to 6
- key_cache: bfloat16 [8, 32768, 1024], P('rows', 'seq'), may hold values from -16 to 16
- value_cache: bfloat16 [8, 32768, 1024], P('rows', 'seq'), may hold values from -6 to 6
- lengths: int32 [8], replicated, may hold values from 2 to 32766, as said below
- row_slot: int32 [8], replicated, may hold values from 0 to 7, each once
Outputs:
- attended: bfloat16 [2, 8, 8192], P(None, None, 'seq')
Inputs may be any that keep to these rules, and one draw needn't show every extreme that they name: `lengths`: every request has at least two cached tokens and room for 2 more; some request has exactly 32766.
All inputs are finite; a program needn't handle non-finite values.
Results may differ from a plain program's by a relative error of at most 0.0085.
Values may be sent and summed in bfloat16 or wider, within the bound.
A program may use at most 192 MiB of HBM per device.

v0:
```python
import jax
import jax.numpy as jnp
from jax import lax
from jax.sharding import PartitionSpec as P

HEAD_DIM = 128


def local(queries, new_keys, new_values, key_cache, value_cache, lengths, row_slot):
    gathered_queries, gathered_keys, gathered_values = (
        lax.all_gather(queries, "seq", axis=2, tiled=True),
        lax.all_gather(new_keys, "seq", axis=2, tiled=True),
        lax.all_gather(new_values, "seq", axis=2, tiled=True),
    )
    steps = gathered_queries.shape[0]
    rows_dev, ctx_dev, kv_feat = key_cache.shape
    features = gathered_queries.shape[2]
    heads = features // HEAD_DIM
    kv_heads = kv_feat // HEAD_DIM
    group = heads // kv_heads
    width = features // lax.axis_size("seq")
    group_index = lax.axis_index("rows")
    seq_index = lax.axis_index("seq")
    slots = group_index * rows_dev + jnp.arange(rows_dev, dtype=jnp.int32)
    owner_match = row_slot[None, :] == slots[:, None]
    owner_selector = owner_match.astype(jnp.bfloat16)
    shard_queries = jnp.einsum(
        "no,doa->dna", owner_selector, gathered_queries, preferred_element_type=jnp.float32
    ).astype(jnp.bfloat16)
    shard_keys = jnp.einsum(
        "no,doa->dna", owner_selector, gathered_keys, preferred_element_type=jnp.float32
    ).astype(jnp.bfloat16)
    shard_values = jnp.einsum(
        "no,doa->dna", owner_selector, gathered_values, preferred_element_type=jnp.float32
    ).astype(jnp.bfloat16)
    local_len = jnp.sum(jnp.where(owner_match, lengths[None, :], 0), axis=1)
    positions = seq_index * ctx_dev + jnp.arange(ctx_dev, dtype=jnp.int32)
    keys = key_cache
    values = value_cache
    for step in range(steps):
        hit = (positions[None, :] == (local_len + step)[:, None])[:, :, None]
        keys = jnp.where(hit, shard_keys[step][:, None, :], keys)
        values = jnp.where(hit, shard_values[step][:, None, :], values)
    query_five = shard_queries.reshape(steps, rows_dev, kv_heads, group, HEAD_DIM)
    key_four = keys.reshape(rows_dev, ctx_dev, kv_heads, HEAD_DIM)
    value_four = values.reshape(rows_dev, ctx_dev, kv_heads, HEAD_DIM).astype(jnp.float32)
    scores = jnp.einsum(
        "tjkgd,jnkd->tjkgn", query_five, key_four, preferred_element_type=jnp.float32
    )
    scores = scores * HEAD_DIM ** (-0.5)
    limit = local_len[None, :] + 1 + jnp.arange(steps, dtype=jnp.int32)[:, None]
    valid = (positions[None, None, :] < limit[:, :, None])[:, :, None, None, :]
    masked = jnp.where(valid, scores, jnp.float32(-1e30))
    local_max = jnp.max(masked, axis=-1).reshape(steps, rows_dev, heads)
    start = seq_index * width
    top = lax.pmax(local_max, "seq")
    top_five = top.reshape(steps, rows_dev, kv_heads, group)
    expo = jnp.where(valid, jnp.exp(masked - top_five[..., None]), jnp.float32(0.0))
    total = jnp.sum(expo, axis=-1).reshape(steps, rows_dev, heads)
    summed = jnp.einsum("tjkgn,jnkd->tjkgd", expo, value_four, precision=lax.Precision.HIGHEST)
    total, summed = (total, summed.reshape(steps, rows_dev, heads, HEAD_DIM))
    totals, sums = lax.psum((total, summed), "seq")
    whole = (sums / totals[..., None]).reshape(steps, rows_dev, features)
    owned_partial = lax.dynamic_slice_in_dim(whole, start, width, 2)
    placed = jnp.einsum(
        "va,qvw->qaw",
        owner_match.astype(jnp.float32),
        owned_partial,
        precision=lax.Precision.HIGHEST,
    )
    return lax.psum(placed, "rows").astype(jnp.bfloat16)


def solution(mesh):
    in_specs = (
        P(None, None, "seq"),
        P(None, None, "seq"),
        P(None, None, "seq"),
        P("rows", "seq", None),
        P("rows", "seq", None),
        P(),
        P(),
    )
    out_specs = P(None, None, "seq")
    return jax.shard_map(local, mesh=mesh, in_specs=in_specs, out_specs=out_specs, check_vma=False)
```

profile of v0, /device:TPU:1, one launch (start us, length us, event | category | flops | bytes accessed | tf_op | source)
XLA Modules:
  0.0 2110.9 jit_solution(10674545604658989025)
XLA Ops:
  6.5 0.7 compare_bitcast_fusion
  7.3 0.9 fusion.28
  8.3 0.8 copy.27
  9.0 296.6 %all_gather.10 = bf16[2,8,1024]{1,0,2:T(2,128)(2,1)S(1)} all-gather(bf16[2,8,8]{1,0,2:T(2,128)(2,1)S(1)} %copy.27), channel_id=1, replica_groups=mesh['seq'=128,'rows'=2] {'seq'}, dimensions={2}, use_global_device_ids=true | all-gather | bytes 33024 | tf_op jit(solution)/shard_map/all_gather | solution.py:12
  305.6 0.2 fusion.19
  305.9 0.8 copy.25
  306.7 285.6 %all_gather.9 = bf16[2,8,1024]{1,0,2:T(2,128)(2,1)S(1)} all-gather(bf16[2,8,8]{1,0,2:T(2,128)(2,1)S(1)} %copy.25), channel_id=1, replica_groups=mesh['seq'=128,'rows'=2] {'seq'}, dimensions={2}, use_global_device_ids=true | all-gather | bytes 33024 | tf_op jit(solution)/shard_map/all_gather | solution.py:13
  592.2 0.2 fusion.18
  592.5 2.5 select_select_fusion
  595.0 0.6 copy.42
  595.6 1.5 bitcast_bitcast_fusion.1
  597.2 308.6 %all_gather.11 = bf16[2,8,8192]{1,0,2:T(2,128)(2,1)S(1)} all-gather(bf16[2,8,64]{1,0,2:T(2,128)(2,1)S(1)} %copy.29), channel_id=1, replica_groups=mesh['seq'=128,'rows'=2] {'seq'}, dimensions={2}, use_global_device_ids=true | all-gather | bytes 264192 | tf_op jit(solution)/shard_map/all_gather | solution.py:11
  905.8 1.2 fusion
  907.2 0.6 copy.43
  908.0 0.8 fusion.31
  908.8 571.6 %pmax.7 = f32[2,4,8,8]{3,0,2,1:T(2,128)S(1)} all-reduce(f32[2,4,8,8]{3,0,2,1:T(2,128)S(1)} %get-tuple-element.13), channel_id=1, replica_groups=mesh['seq'=128,'rows'=2] {'seq'}, use_global_device_ids=true, to_apply=%region_2.3 | all-reduce | flops 512 | bytes 4096 | tf_op jit(solution)/shard_map/pmax | solution.py:56
  1480.4 1.1 fusion.15
  1481.5 0.7 copy.69
  1482.2 0.3 fusion.22
  1482.6 287.1 %psum.22 = f32[2,4,64]{2,1,0:T(4,128)S(1)} all-reduce(f32[2,4,64]{2,1,0:T(4,128)S(1)} %reshape.128), channel_id=1, replica_groups=mesh['seq'=128,'rows'=2] {'seq'}, use_global_device_ids=true, to_apply=%region_5.6 | all-reduce | flops 512 | bytes 4096 | tf_op jit(solution)/shard_map/psum | solution.py:62
  1769.7 186.4 %all-reduce.2.cloned.1.call-done = f32[2,4,64,128]{3,2,1,0:T(8,128)} async-done(((f32[2,4,64,128]{3,2,1,0:T(8,128)}), f32[2,4,64,128]{3,2,1,0:T(8,128)}) %all-reduce.2.cloned.1.call-update) | async-done | bytes 262160 | tf_op jit(solution)/shard_map/psum | solution.py:62
  1956.1 1.1 broadcast_divide_fusion
  1957.3 0.2 convolution_bitcast_fusion
  1957.5 146.5 %psum.23 = bf16[2,8,64]{2,1,0:T(8,128)(2,1)} all-reduce(f32[2,8,64]{2,1,0:T(8,128)S(1)} %convolution_bitcast_fusion), channel_id=1, replica_groups=mesh['seq'=128,'rows'=2] {'rows'}, use_global_device_ids=true, to_apply=%region_6.7 | all-reduce | flops 1024 | bytes 6144 | tf_op jit(solution)/shard_map/psum | solution.py:71
  (20 shorter events, 0.9 us)
Async XLA Ops:
  6.5 1949.6 %all-reduce.2.cloned.1.call-start = ((), (), s32[]{:S(2)}) async-start(), calls=%async_computation | async-start | bytes 524288 | tf_op jit(solution)/shard_map/psum | solution.py:62
  595.6 1.5 copy-start.1
  908.0 572.4 %copy-start = (bf16[4,256,8,128,1]{3,2,1,0,4:T(8,128)(2,1)S(1)}, bf16[4,256,8,128,1]{3,2,1,0,4:T(8,128)(2,1)}, u32[]{:S(2)}) copy-start(bf16[4,256,8,128,1]{3,2,1,0,4:T(8,128)(2,1)} %bitcast_bitcast_fusion.1) | copy-start | bytes 6291460
Sparse Core Ops, SparseCore 0:
  1482.3 473.7 all-reduce.1
where the time goes:
time: 2110 us
  blocking collectives  1900 us (90%)
  waiting for transfers between devices  186 us (9%)
    pmax x1, blocking collectives, local(): top = lax.pmax(local_max, 'seq')  572 us
    all_gather x1, blocking collectives, local(): lax.all_gather(queries, 'seq', axis=2, tiled=True)  309 us
    all_gather x1, blocking collectives, local(): lax.all_gather(new_keys, 'seq', axis=2, tiled=True)  297 us
    psum x1, blocking collectives, local(): totals, sums = lax.psum((total, summed), 'seq')  287 us
    all_gather x1, blocking collectives, local(): lax.all_gather(new_values, 'seq', axis=2, tiled=True)  286 us
    psum x1, waiting for transfers between devices, local(): totals, sums = lax.psum((total, summed), 'seq')  186 us
    psum x1, blocking collectives, local(): return lax.psum(placed, 'rows').astype(jnp.bfloat16)  147 us
  transfers between devices with their start and end apart: 1, of which 1 were waited for; matrix products, arithmetic and copies ran while one was open for 0% of the time, Pallas kernels for 0%

commit v1 on v0

v1 whole, which is shorter than its diff:
```python
import functools

import jax
import jax.numpy as jnp
from jax import lax
from jax.experimental import pallas as pl
from jax.experimental.pallas import tpu as pltpu
from jax.sharding import PartitionSpec as P

NX, NZ, NY = 4, 8, 4
HEAD_DIM = 128
SLOTS = 4
CTX = 256
NEG = -1e30
SCALE = HEAD_DIM**-0.5 * 1.4426950408889634
MESH = pl.DeviceIdType.MESH
F32, BF16, I32 = jnp.float32, jnp.bfloat16, jnp.int32


def iota(shape, dim):
    return lax.broadcasted_iota(I32, shape, dim)


def kernel(
    q_hbm, nk_hbm, nv_hbm, k_hbm, v_hbm, len_ref, slot_ref, out_ref,
    q_in, nk_in, nv_in, k_buf, v_buf,
    q_y, kv_y, kv_z, q_all,
    o_x, ml_x, o_x_in, ml_x_in, o_z, ml_z, o_z_in, ml_z_in, fin, fin_in,
    in_sem, cache_sem,
    qy_s, qy_r, kvy_s, kvy_r, kvz_s, kvz_r, qz_s, qz_r, qx_s, qx_r,
    ox_s, ox_r, mx_s, mx_r, oz_s, oz_r, mz_s, mz_r, f_s, f_r,
):
    seq, core = lax.axis_index("seq"), lax.axis_index("rows")
    y = lax.rem(seq, NY)
    z = lax.rem(lax.div(seq, NY), NZ)
    x = lax.div(seq, NY * NZ)

    def at(xx, zz, yy, cc):
        return {"seq": (xx * NZ + zz) * NY + yy, "rows": cc}

    def remote(src, dst, send, recv, target):
        return pltpu.make_async_remote_copy(
            src_ref=src, dst_ref=dst, send_sem=send, recv_sem=recv, device_id=target, device_id_type=MESH
        )

    y_peer = [at(x, z, lax.rem(y + d, NY), core) for d in range(NY)]
    z_peer = [at(x, lax.rem(z + d, NZ), y, core) for d in range(NZ)]
    x_peer = [at(lax.rem(x + d, NX), z, y, core) for d in range(NX)]
    c_peer = [at(x, z, lax.rem(y + d, NY), 1 - core) for d in range(NY)]
    half = lax.div(z, 4)
    zq = lax.rem(z, 4)
    h_peer = [at(x, half * 4 + lax.rem(zq + d, 4), y, core) for d in range(4)]

    loads = [
        pltpu.make_async_copy(q_hbm, q_in, in_sem.at[0]),
        pltpu.make_async_copy(nk_hbm, nk_in, in_sem.at[1]),
        pltpu.make_async_copy(nv_hbm, nv_in, in_sem.at[2]),
    ]
    for c in loads:
        c.start()
    k_loads = [pltpu.make_async_copy(k_hbm.at[s], k_buf.at[s], cache_sem.at[s]) for s in range(SLOTS)]
    v_loads = [pltpu.make_async_copy(v_hbm.at[s], v_buf.at[s], cache_sem.at[SLOTS + s]) for s in range(SLOTS)]
    for c in k_loads + v_loads:
        c.start()

    barrier = pltpu.get_barrier_semaphore()
    peers = y_peer[1:] + z_peer[1:] + x_peer[1:] + c_peer
    for p in peers:
        pl.semaphore_signal(barrier, inc=1, device_id=p, device_id_type=MESH)

    slots = [slot_ref[r] for r in range(8)]
    for c in loads:
        c.wait()

    def by_slot(ref):
        width = ref.shape[2]
        row = iota((8, width), 0)
        wanted = core * SLOTS + lax.rem(row, 4)
        acc = jnp.zeros((8, width), F32)
        for t in range(2):
            whole = ref[t].astype(F32)
            for r in range(8):
                hit = (wanted == slots[r]) & (lax.div(row, 4) == t)
                acc = jnp.where(hit, jnp.broadcast_to(whole[r : r + 1], (8, width)), acc)
        return acc

    mine = by_slot(q_in)
    wide = jnp.concatenate([mine, mine], axis=1)
    wide = jnp.where(lax.div(iota((8, 128), 1), 64) == lax.rem(y, 2), wide, 0.0)
    tile = jnp.concatenate([jnp.where(lax.div(y, 2) == hh, wide, 0.0) for hh in range(2)], axis=0)
    q_y[0] = tile.astype(BF16)

    pl.semaphore_wait(barrier, len(peers))

    qy = [remote(q_y.at[0], q_y.at[d], qy_s.at[d], qy_r.at[d], y_peer[d]) for d in range(1, NY)]
    for c in qy:
        c.start()

    lane = iota((8, 128), 1)
    base = zq * 32 + y * 8
    for i, ref in enumerate((nk_in, nv_in)):
        part = by_slot(ref)
        acc = jnp.zeros((8, 128), F32)
        for f in range(8):
            acc = jnp.where(lane == base + f, jnp.broadcast_to(part[:, f : f + 1], (8, 128)), acc)
        kv_y[0, 8 * i : 8 * i + 8] = acc
    kvy = [remote(kv_y.at[0], kv_y.at[d], kvy_s.at[d], kvy_r.at[d], y_peer[d]) for d in range(1, NY)]
    for c in kvy:
        c.start()

    for c in qy:
        c.wait_recv()
    own_q = (q_y[0] + q_y[1]) + (q_y[2] + q_y[3])
    q_all[x, z] = own_q

    qz = [remote(q_all.at[x, z], q_all.at[x, z], qz_s.at[d], qz_r.at[d], z_peer[d]) for d in range(1, NZ)]
    for c in qz:
        c.start()
    for c in kvy:
        c.wait_recv()
    kv_z[0] = (kv_y[0] + kv_y[1]) + (kv_y[2] + kv_y[3])
    kvz = [remote(kv_z.at[0], kv_z.at[d], kvz_s.at[d], kvz_r.at[d], h_peer[d]) for d in range(1, 4)]
    for c in kvz:
        c.start()

    def z_in(d):
        zz = lax.rem(z + NZ - d, NZ)
        return remote(q_all.at[x, zz], q_all.at[x, zz], qz_s.at[d], qz_r.at[d], z_peer[d])

    for d in range(1, NZ):
        z_in(d).wait_recv()

    qx = [remote(q_all.at[x], q_all.at[x], qx_s.at[d], qx_r.at[d], x_peer[d]) for d in range(1, NX)]
    for c in qx:
        c.start()

    def x_in(d):
        xx = lax.rem(x + NX - d, NX)
        return remote(q_all.at[xx], q_all.at[xx], qx_s.at[d], qx_r.at[d], x_peer[d])

    slot_of = lax.rem(iota((64, CTX), 0), SLOTS)
    limit = jnp.zeros((64, CTX), I32)
    for s in range(SLOTS):
        n = jnp.int32(0)
        for r in range(8):
            n = n + jnp.where(slots[r] == core * SLOTS + s, len_ref[r], 0)
        limit = jnp.where(slot_of == s, n, limit)
    valid = seq * CTX + iota((64, CTX), 1) < limit
    slot_out = lax.rem(iota((64, HEAD_DIM), 0), SLOTS)
    lane16 = iota((16, 128), 1)

    for c in k_loads + v_loads:
        c.wait()

    def attend(xb, slot):
        ml = jnp.zeros((16, 128), F32)
        for j in range(2):
            cols = pl.ds(pl.multiple_of((xb * 2 + j) * HEAD_DIM, HEAD_DIM), HEAD_DIM)
            q = q_all[xb, 4 * j : 4 * j + 4].reshape(64, HEAD_DIM)
            scores = None
            for s in range(SLOTS):
                part = lax.dot_general(q, k_buf[s, :, cols], (((1,), (1,)), ((), ())), preferred_element_type=F32)
                scores = part if s == 0 else jnp.where(slot_of == s, part, scores)
            scores = jnp.where(valid, scores * SCALE, NEG)
            top = jnp.max(scores, axis=1, keepdims=True)
            p = jnp.where(valid, jnp.exp2(scores - top), 0.0)
            total = jnp.sum(p, axis=1, keepdims=True)
            p = p.astype(BF16)
            out = None
            for s in range(SLOTS):
                part = jnp.dot(p, v_buf[s, :, cols], preferred_element_type=F32)
                out = part if s == 0 else jnp.where(slot_out == s, part, out)
            o_x[slot, 4 * j : 4 * j + 4] = out.astype(BF16).reshape(4, 16, HEAD_DIM)
            for zz in range(4):
                rows = slice(16 * zz, 16 * zz + 16)
                ml = jnp.where(lane16 == 4 * j + zz, top[rows], ml)
                ml = jnp.where(lane16 == 64 + 4 * j + zz, total[rows], ml)
        ml_x[slot] = ml

    back = []
    for d in range(1, NX):
        x_in(d).wait_recv()
        attend(lax.rem(x + NX - d, NX), d)
        target = x_peer[NX - d]
        back.append(remote(o_x.at[d], o_x_in.at[d], ox_s.at[d], ox_r.at[d], target))
        back.append(remote(ml_x.at[d], ml_x_in.at[d], mx_s.at[d], mx_r.at[d], target))
        back[-2].start()
        back[-1].start()
    attend(x, 0)

    for c in kvz:
        c.wait_recv()
    kv = (kv_z[0] + kv_z[1]) + (kv_z[2] + kv_z[3])
    row8 = iota((8, 128), 0)

    def spread(block):
        turned = jnp.concatenate([block[4:8], block[0:4]], axis=0)
        return jnp.where(row8 < 4, block, turned), jnp.where(row8 < 4, turned, block)

    key0, key1 = spread(kv[0:8])
    val0, val1 = spread(kv[8:16])
    both = lambda a: jnp.concatenate([a, a], axis=0)
    qf = own_q.astype(F32)
    second = lax.rem(lax.div(iota((16, 1), 0), 4), 2) == 1
    here = y == 0
    s0 = jnp.sum(qf * both(key0), axis=1, keepdims=True) * SCALE
    s1 = jnp.where(second, jnp.sum(qf * both(key1), axis=1, keepdims=True) * SCALE, NEG)
    new_top = jnp.maximum(s0, s1)
    p0 = jnp.exp2(s0 - new_top)
    p1 = jnp.where(second, jnp.exp2(s1 - new_top), 0.0)
    new_out = p0 * both(val0) + p1 * both(val1)
    new_top = jnp.where(here, new_top, NEG)
    new_total = jnp.where(here, p0 + p1, 0.0)
    new_out = jnp.where(here, new_out, 0.0)

    for c in back:
        c.wait_recv()
    mls = [ml_x[0]] + [ml_x_in[d] for d in range(1, NX)]

    def weigh(mls):
        top = functools.reduce(jnp.maximum, mls)
        factors = [jnp.exp2(m - top) for m in mls]
        total = sum(pltpu.roll(f, 64, 1) * m for f, m in zip(factors, mls))
        return factors, jnp.where(lane16 < 64, top, total)

    factors, ml = weigh(mls)
    ml_z[...] = ml
    for zz in range(NZ):
        acc = factors[0][:, zz : zz + 1] * o_x[0, zz].astype(F32)
        for d in range(1, NX):
            acc = acc + factors[d][:, zz : zz + 1] * o_x_in[d, zz].astype(F32)
        o_z[zz] = acc.astype(BF16)

    oz, mz = [], []
    for d in range(1, NZ):
        zz = lax.rem(z + d, NZ)
        oz.append(remote(o_z.at[zz], o_z_in.at[d], oz_s.at[d], oz_r.at[d], z_peer[d]))
        mz.append(remote(ml_z, ml_z_in.at[d], mz_s.at[d], mz_r.at[d], z_peer[d]))
        oz[-1].start()
        mz[-1].start()
    for c in oz + mz:
        c.wait_recv()
    mls = [ml] + [ml_z_in[d] for d in range(1, NZ)]
    outs = [o_z[z]] + [o_z_in[d] for d in range(1, NZ)]

    def column(tile, at_lane):
        return jnp.sum(jnp.where(lane16 == at_lane, tile, 0.0), axis=1, keepdims=True)

    factors, ml = weigh(mls)
    top, total = column(ml, z), column(ml, z + 64)
    acc = sum(column(f, z) * o.astype(F32) for f, o in zip(factors, outs))
    best = jnp.maximum(top, new_top)
    old_factor, new_factor = jnp.exp2(top - best), jnp.exp2(new_top - best)
    acc = old_factor * acc + new_factor * new_out
    total = old_factor * total + new_factor * new_total

    for yy in range(NY):
        rows = slice(8 * (yy // 2), 8 * (yy // 2) + 8)
        part = acc[rows]
        if yy % 2:
            part = pltpu.roll(part, 64, 1)
        fin[yy] = jnp.where(lane < 64, part, jnp.where(lane < 96, best[rows], total[rows]))
    f = []
    for d in range(NY):
        for other in range(2):
            if d or other:
                yy = lax.rem(y + d, NY)
                i = other * NY + d
                f.append(remote(fin.at[yy], fin_in.at[i], f_s.at[i], f_r.at[i], (c_peer if other else y_peer)[d]))
    for c in f:
        c.start()
    for c in f:
        c.wait_recv()

    parts = []
    for other in range(2):
        tiles = [fin[y] if i == 0 else fin_in[i] for i in range(other * NY, other * NY + NY)]
        top = functools.reduce(jnp.maximum, tiles)
        acc = sum(jnp.exp2(t - top)[:, 64:65] * t for t in tiles)
        parts.append(acc[:, :64] / acc[:, 96:97])
    row = iota((8, 64), 0)
    slot_row = jnp.zeros((8, 64), I32)
    for r in range(8):
        slot_row = jnp.where(row == r, slots[r], slot_row)
    for t in range(2):
        result = jnp.zeros((8, 64), F32)
        for other in range(2):
            group = core + other - 2 * core * other
            for s in range(SLOTS):
                i = t * 4 + s
                found = slot_row == group * SLOTS + s
                result = jnp.where(found, jnp.broadcast_to(parts[other][i : i + 1], (8, 64)), result)
        out_ref[t] = result.astype(BF16)

    for c in qy + kvy + qz + kvz + qx + back + oz + mz + f:
        c.wait_send()


def local(queries, new_keys, new_values, key_cache, value_cache, lengths, row_slot):
    anywhere = pl.BlockSpec(memory_space=pl.ANY)
    scalars = pl.BlockSpec(memory_space=pltpu.SMEM)
    sem = pltpu.SemaphoreType.DMA
    return pl.pallas_call(
        kernel,
        out_shape=jax.ShapeDtypeStruct(queries.shape, BF16),
        in_specs=[anywhere] * 5 + [scalars] * 2,
        out_specs=pl.BlockSpec(memory_space=pltpu.VMEM),
        scratch_shapes=[
            pltpu.VMEM(queries.shape, BF16),
            pltpu.VMEM(new_keys.shape, BF16),
            pltpu.VMEM(new_values.shape, BF16),
            pltpu.VMEM(key_cache.shape, BF16),
            pltpu.VMEM(value_cache.shape, BF16),
            pltpu.VMEM((NY, 16, 128), BF16),
            pltpu.VMEM((NY, 16, 128), F32),
            pltpu.VMEM((4, 16, 128), F32),
            pltpu.VMEM((NX, NZ, 16, 128), BF16),
            pltpu.VMEM((NX, NZ, 16, 128), BF16),
            pltpu.VMEM((NX, 16, 128), F32),
            pltpu.VMEM((NX, NZ, 16, 128), BF16),
            pltpu.VMEM((NX, 16, 128), F32),
            pltpu.VMEM((NZ, 16, 128), BF16),
            pltpu.VMEM((16, 128), F32),
            pltpu.VMEM((NZ, 16, 128), BF16),
            pltpu.VMEM((NZ, 16, 128), F32),
            pltpu.VMEM((NY, 8, 128), F32),
            pltpu.VMEM((2 * NY, 8, 128), F32),
            sem((3,)), sem((2 * SLOTS,)),
            sem((NY,)), sem((NY,)), sem((NY,)), sem((NY,)), sem((4,)), sem((4,)),
            sem((NZ,)), sem((NZ,)), sem((NX,)), sem((NX,)),
            sem((NX,)), sem((NX,)), sem((NX,)), sem((NX,)),
            sem((NZ,)), sem((NZ,)), sem((NZ,)), sem((NZ,)),
            sem((2 * NY,)), sem((2 * NY,)),
        ],
        compiler_params=pltpu.CompilerParams(
            collective_id=0, has_side_effects=True, vmem_limit_bytes=48 * 1024 * 1024
        ),
    )(queries, new_keys, new_values, key_cache, value_cache, lengths, row_slot)


def solution(mesh):
    in_specs = (
        P(None, None, "seq"),
        P(None, None, "seq"),
        P(None, None, "seq"),
        P("rows", "seq", None),
        P("rows", "seq", None),
        P(),
        P(),
    )
    out_specs = P(None, None, "seq")
    return jax.shard_map(local, mesh=mesh, in_specs=in_specs, out_specs=out_specs, check_vma=False)
```

time: 2110 us -> 46.2 us (0.02)
  blocking collectives: 1900 us -> 0 us
  waiting for transfers between devices: 186 us -> 0 us
  Pallas kernels: 0 us -> 38.8 us
    all_gather x3 -> x0, blocking collectives: 891 us -> none  [the longest x1 309 us: local(): lax.all_gather(queries, 'seq', axis=2, tiled=True)]
    pmax x1 -> x0, blocking collectives: 572 us -> none  [local(): top = lax.pmax(local_max, 'seq')]
    psum x2 -> x0, blocking collectives: 434 us -> none  [the longest x1 287 us: local(): totals, sums = lax.psum((total, summed), 'seq')]
    psum x1 -> x0, waiting for transfers between devices: 186 us -> none  [local(): totals, sums = lax.psum((total, summed), 'seq')]
    pallas_call x0 -> x1, Pallas kernels: none -> 38.8 us  [local(): pl.pallas_call(kernel, out_shape=jax.ShapeDtypeStruct(queries.shape, BF16...]
  transfers between devices with their start and end apart: 1 -> 0, of which waited for: 1 -> 0; matrix products, arithmetic and copies ran while one was open for 0% -> 0% of each run, Pallas kernels for 0% -> 0%
where the time goes in v1:
time: 46.2 us; the launch traced here: 45.9 us
  Pallas kernels  38.8 us (84%)
  local copies, waits for them, and re-layouts  7.14 us (15%)
    pallas_call x1, Pallas kernels, local(): pl.pallas_call(kernel, out_shape=jax.ShapeDtypeStruct(queries.shape, BF16...  38.8 us
    unnamed x15, local copies, waits for them, and re-layouts  7.14 us

profile of v1, /device:TPU:1, one launch (start us, length us, event | category | flops | bytes accessed | tf_op | source)
XLA Modules:
  0.0 45.9 jit_solution(14824934464157540934)
XLA Ops:
  0.0 0.0 copy-start
  0.0 1.6 %copy-done = bf16[4,256,1024]{2,1,0:T(8,128)(2,1)S(1)} copy-done((bf16[4,256,1024]{2,1,0:T(8,128)(2,1)S(1)}, bf16[4,256,1024]{2,1,0:T(8,128)(2,1)}, u32[]{:S(2)}) %copy-start) | copy-done | bytes 2097176
  1.6 0.0 copy-start.1
  1.6 1.6 %copy-done.1 = bf16[4,256,1024]{2,1,0:T(8,128)(2,1)S(1)} copy-done((bf16[4,256,1024]{2,1,0:T(8,128)(2,1)S(1)}, bf16[4,256,1024]{2,1,0:T(8,128)(2,1)}, u32[]{:S(2)}) %copy-start.1) | copy-done | bytes 2097176
  3.2 0.0 copy-start.2
  3.2 0.7 %copy-done.2 = bf16[2,8,64]{2,1,0:T(8,128)(2,1)S(1)} copy-done((bf16[2,8,64]{2,1,0:T(8,128)(2,1)S(1)}, bf16[2,8,64]{2,1,0:T(8,128)(2,1)}, u32[]{:S(2)}) %copy-start.2) | copy-done | bytes 2072
  3.9 0.0 copy-start.3
  3.9 0.7 %copy-done.3 = bf16[2,8,8]{2,1,0:T(8,128)(2,1)S(1)} copy-done((bf16[2,8,8]{2,1,0:T(8,128)(2,1)S(1)}, bf16[2,8,8]{2,1,0:T(8,128)(2,1)}, u32[]{:S(2)}) %copy-start.3) | copy-done | bytes 280
  4.6 0.0 copy-start.4
  4.6 0.7 %copy-done.4 = bf16[2,8,8]{2,1,0:T(8,128)(2,1)S(1)} copy-done((bf16[2,8,8]{2,1,0:T(8,128)(2,1)S(1)}, bf16[2,8,8]{2,1,0:T(8,128)(2,1)}, u32[]{:S(2)}) %copy-start.4) | copy-done | bytes 280
  5.2 0.0 copy-start.5
  5.2 0.7 %copy-done.5 = s32[8]{0:T(128)S(1)} copy-done((s32[8]{0:T(128)S(1)}, s32[8]{0:T(128)}, u32[]{:S(2)}) %copy-start.5) | copy-done | bytes 56
  5.9 0.0 copy-start.6
  5.9 0.7 %copy-done.6 = s32[8]{0:T(128)S(1)} copy-done((s32[8]{0:T(128)S(1)}, s32[8]{0:T(128)}, u32[]{:S(2)}) %copy-start.6) | copy-done | bytes 56
  6.6 38.8 %shard_map.73 = bf16[2,8,64]{2,1,0:T(8,128)(2,1)S(1)} custom-call(bf16[2,8,64]{2,1,0:T(8,128)(2,1)S(1)} %copy-done.2, bf16[2,8,8]{2,1,0:T(8,128)(2,1)S(1)} %copy-done.3, bf16[2,8,8]{2,1,0:T(8,128)(2,1)S(1)} %copy-done.4, bf16[4,256,1024]{2,1,0:T(8,128)(2,1)S(1)} %copy-done, bf16[4,256,1024]{2,1,0:T(8,128)(2,1)S(1)} %copy-done.1, s32[8]{0:T(128)S(1)} %copy-done.5, ...), custom_call_target="tpu_custom_call" | custom-call | tf_op jit(solution)/shard_map/pallas_call | solution.py:303
  45.3 0.6 %copy.9 = bf16[2,8,64]{2,1,0:T(8,128)(2,1)} copy(bf16[2,8,64]{2,1,0:T(8,128)(2,1)S(1)} %shard_map.73) | data formatting | bytes 4096
Async XLA Ops:
  0.0 1.6 %copy-start = (bf16[4,256,1024]{2,1,0:T(8,128)(2,1)S(1)}, bf16[4,256,1024]{2,1,0:T(8,128)(2,1)}, u32[]{:S(2)}) copy-start(bf16[4,256,1024]{2,1,0:T(8,128)(2,1)} %k_hbm.1) | copy-start | bytes 6291460
  1.6 1.6 %copy-start.1 = (bf16[4,256,1024]{2,1,0:T(8,128)(2,1)S(1)}, bf16[4,256,1024]{2,1,0:T(8,128)(2,1)}, u32[]{:S(2)}) copy-start(bf16[4,256,1024]{2,1,0:T(8,128)(2,1)} %v_hbm.1) | copy-start | bytes 6291460
  3.2 0.7 %copy-start.2 = (bf16[2,8,64]{2,1,0:T(8,128)(2,1)S(1)}, bf16[2,8,64]{2,1,0:T(8,128)(2,1)}, u32[]{:S(2)}) copy-start(bf16[2,8,64]{2,1,0:T(8,128)(2,1)} %q_hbm.1) | copy-start | bytes 6148
  3.9 0.7 %copy-start.3 = (bf16[2,8,8]{2,1,0:T(8,128)(2,1)S(1)}, bf16[2,8,8]{2,1,0:T(8,128)(2,1)}, u32[]{:S(2)}) copy-start(bf16[2,8,8]{2,1,0:T(8,128)(2,1)} %nk_hbm.1) | copy-start | bytes 772
  4.6 0.7 %copy-start.4 = (bf16[2,8,8]{2,1,0:T(8,128)(2,1)S(1)}, bf16[2,8,8]{2,1,0:T(8,128)(2,1)}, u32[]{:S(2)}) copy-start(bf16[2,8,8]{2,1,0:T(8,128)(2,1)} %nv_hbm.1) | copy-start | bytes 772
  5.2 0.7 %copy-start.5 = (s32[8]{0:T(128)S(1)}, s32[8]{0:T(128)}, u32[]{:S(2)}) copy-start(s32[8]{0:T(128)} %len_ref.1) | copy-start | bytes 100
  5.9 0.7 %copy-start.6 = (s32[8]{0:T(128)S(1)}, s32[8]{0:T(128)}, u32[]{:S(2)}) copy-start(s32[8]{0:T(128)} %slot_ref.1) | copy-start | bytes 100

commit v2 on v1

--- a/solution.py
+++ b/solution.py
@@ -22,8 +22,8 @@
 
 
 def kernel(
-    q_hbm, nk_hbm, nv_hbm, k_hbm, v_hbm, len_ref, slot_ref, out_ref,
-    q_in, nk_in, nv_in, k_buf, v_buf,
+    q_hbm, nk_hbm, nv_hbm, k_hbm, v_hbm, len_hbm, slot_hbm, out_ref,
+    q_in, nk_in, nv_in, len_ref, slot_ref, k_buf, v_buf,
     q_y, kv_y, kv_z, q_all,
     o_x, ml_x, o_x_in, ml_x_in, o_z, ml_z, o_z_in, ml_z_in, fin, fin_in,
     in_sem, cache_sem,
@@ -55,6 +55,8 @@
         pltpu.make_async_copy(q_hbm, q_in, in_sem.at[0]),
         pltpu.make_async_copy(nk_hbm, nk_in, in_sem.at[1]),
         pltpu.make_async_copy(nv_hbm, nv_in, in_sem.at[2]),
+        pltpu.make_async_copy(slot_hbm, slot_ref, in_sem.at[3]),
+        pltpu.make_async_copy(len_hbm, len_ref, in_sem.at[4]),
     ]
     for c in loads:
         c.start()
@@ -68,9 +70,9 @@
     for p in peers:
         pl.semaphore_signal(barrier, inc=1, device_id=p, device_id_type=MESH)
 
-    slots = [slot_ref[r] for r in range(8)]
     for c in loads:
         c.wait()
+    slots = [slot_ref[r] for r in range(8)]
 
     def by_slot(ref):
         width = ref.shape[2]
@@ -297,18 +299,18 @@
 
 
 def local(queries, new_keys, new_values, key_cache, value_cache, lengths, row_slot):
-    anywhere = pl.BlockSpec(memory_space=pl.ANY)
-    scalars = pl.BlockSpec(memory_space=pltpu.SMEM)
     sem = pltpu.SemaphoreType.DMA
     return pl.pallas_call(
         kernel,
         out_shape=jax.ShapeDtypeStruct(queries.shape, BF16),
-        in_specs=[anywhere] * 5 + [scalars] * 2,
+        in_specs=[pl.BlockSpec(memory_space=pltpu.HBM)] * 7,
         out_specs=pl.BlockSpec(memory_space=pltpu.VMEM),
         scratch_shapes=[
             pltpu.VMEM(queries.shape, BF16),
             pltpu.VMEM(new_keys.shape, BF16),
             pltpu.VMEM(new_values.shape, BF16),
+            pltpu.SMEM(lengths.shape, I32),
+            pltpu.SMEM(row_slot.shape, I32),
             pltpu.VMEM(key_cache.shape, BF16),
             pltpu.VMEM(value_cache.shape, BF16),
             pltpu.VMEM((NY, 16, 128), BF16),
@@ -325,7 +327,7 @@
             pltpu.VMEM((NZ, 16, 128), F32),
             pltpu.VMEM((NY, 8, 128), F32),
             pltpu.VMEM((2 * NY, 8, 128), F32),
-            sem((3,)), sem((2 * SLOTS,)),
+            sem((5,)), sem((2 * SLOTS,)),
             sem((NY,)), sem((NY,)), sem((NY,)), sem((NY,)), sem((4,)), sem((4,)),
             sem((NZ,)), sem((NZ,)), sem((NX,)), sem((NX,)),
             sem((NX,)), sem((NX,)), sem((NX,)), sem((NX,)),
@@ -333,7 +335,7 @@
             sem((2 * NY,)), sem((2 * NY,)),
         ],
         compiler_params=pltpu.CompilerParams(
-            collective_id=0, has_side_effects=True, vmem_limit_bytes=48 * 1024 * 1024
+            collective_id=0, has_side_effects=True, vmem_limit_bytes=64 * 1024 * 1024
         ),
     )(queries, new_keys, new_values, key_cache, value_cache, lengths, row_slot)
 

time: 46.2 us -> 39.9 us (0.86)
  local copies, waits for them, and re-layouts: 7.14 us -> 1.28 us
    unnamed x15 -> x1, local copies, waits for them, and re-layouts: 7.14 us -> 1.28 us
where the time goes in v2:
time: 39.9 us; the launch traced here: 39.7 us
  Pallas kernels  38.5 us (96%)
  local copies, waits for them, and re-layouts  1.28 us (3%)
    pallas_call x1, Pallas kernels, local(): pl.pallas_call(kernel, out_shape=jax.ShapeDtypeStruct(queries.shape, BF16...  38.5 us
    unnamed x1, local copies, waits for them, and re-layouts  1.28 us

profile of v2, /device:TPU:1, one launch (start us, length us, event | category | flops | bytes accessed | tf_op | source)
XLA Modules:
  0.0 39.7 jit_solution(13941167671290260163)
XLA Ops:
  0.0 38.5 %shard_map.73 = bf16[2,8,64]{2,1,0:T(8,128)(2,1)} custom-call(bf16[2,8,64]{2,1,0:T(8,128)(2,1)} %q_hbm.1, bf16[2,8,8]{2,1,0:T(8,128)(2,1)} %nk_hbm.1, bf16[2,8,8]{2,1,0:T(8,128)(2,1)} %nv_hbm.1, bf16[4,256,1024]{2,1,0:T(8,128)(2,1)} %k_hbm.1, bf16[4,256,1024]{2,1,0:T(8,128)(2,1)} %v_hbm.1, s32[8]{0:T(128)} %len_hbm.1, s32[8]{0:T(128)} %slot_hbm.1), custom_call_target="tpu_custom_call" | custom-call | tf_op jit(solution)/shard_map/pallas_call | solution.py:303
  38.5 1.3 %copy.9 = bf16[2,8,64]{2,1,0:T(8,128)(2,1)} copy(bf16[2,8,64]{2,1,0:T(8,128)(2,1)} %shard_map.73) | data formatting | bytes 4096

commit v3 on v2

v3 whole, which is shorter than its diff:
```python
import functools

import jax
import jax.numpy as jnp
from jax import lax
from jax.experimental import pallas as pl
from jax.experimental.pallas import tpu as pltpu
from jax.sharding import PartitionSpec as P

NX, NZ, NY = 4, 8, 4
HEAD_DIM = 128
SLOTS = 4
CTX = 256
NEG = -1e30
SCALE = HEAD_DIM**-0.5 * 1.4426950408889634
MESH = pl.DeviceIdType.MESH
F32, BF16, I32 = jnp.float32, jnp.bfloat16, jnp.int32


def iota(shape, dim):
    return lax.broadcasted_iota(I32, shape, dim)


def kernel(
    q_hbm, nk_hbm, nv_hbm, k_hbm, v_hbm, len_hbm, slot_hbm, out_ref,
    q_in, nk_in, nv_in, len_ref, slot_ref, k_buf, v_buf,
    new_y, new_z, q_z, q_xy, o_xy, ml_xy, o_in, ml_in, fin, fin_in,
    in_sem, cache_sem,
    ny_s, ny_r, nz_s, nz_r, qz_s, qz_r, qxy_s, qxy_r, o_s, o_r, ml_s, ml_r, f_s, f_r,
):
    seq, core = lax.axis_index("seq"), lax.axis_index("rows")
    y = lax.rem(seq, NY)
    z = lax.rem(lax.div(seq, NY), NZ)
    x = lax.div(seq, NY * NZ)
    pair, half = lax.div(y, 2), lax.rem(y, 2)
    zq = lax.rem(z, 4)

    def at(xx, zz, yy, cc):
        return {"seq": (xx * NZ + zz) * NY + yy, "rows": cc}

    def remote(src, dst, send, recv, target):
        return pltpu.make_async_remote_copy(
            src_ref=src, dst_ref=dst, send_sem=send, recv_sem=recv, device_id=target, device_id_type=MESH
        )

    z_peer = [[at(x, lax.rem(z + d, NZ), y, c) for d in range(NZ)] for c in (core, 1 - core)]
    xy_peer = [[at(lax.rem(x + a, NX), z, lax.rem(y + b, NY), core) for b in range(NY)] for a in range(NX)]
    half_peer = [at(x, z - zq + lax.rem(zq + d, 4), y, core) for d in range(4)]
    others = [(a, b) for a in range(NX) for b in range(NY) if a or b]

    loads = [
        pltpu.make_async_copy(q_hbm, q_in, in_sem.at[0]),
        pltpu.make_async_copy(slot_hbm, slot_ref, in_sem.at[1]),
        pltpu.make_async_copy(nk_hbm, nk_in, in_sem.at[2]),
        pltpu.make_async_copy(nv_hbm, nv_in, in_sem.at[3]),
        pltpu.make_async_copy(len_hbm, len_ref, in_sem.at[4]),
    ]
    for c in loads:
        c.start()

    barrier = pltpu.get_barrier_semaphore()
    peers = z_peer[0][1:] + z_peer[1] + [xy_peer[a][b] for a, b in others]
    for p in peers:
        pl.semaphore_signal(barrier, inc=1, device_id=p, device_id_type=MESH)

    k_loads = [pltpu.make_async_copy(k_hbm.at[s], k_buf.at[s], cache_sem.at[s]) for s in range(SLOTS)]
    v_loads = [pltpu.make_async_copy(v_hbm.at[s], v_buf.at[s], cache_sem.at[SLOTS + s]) for s in range(SLOTS)]
    for c in k_loads + v_loads:
        c.start()
    for c in loads:
        c.wait()
    slots = [slot_ref[r] for r in range(8)]

    def by_slot(ref):
        width = ref.shape[2]
        row = iota((8, width), 0)
        wanted = core * SLOTS + lax.rem(row, 4)
        acc = jnp.zeros((8, width), F32)
        for t in range(2):
            whole = ref[t].astype(F32)
            for r in range(8):
                hit = (wanted == slots[r]) & (lax.div(row, 4) == t)
                acc = jnp.where(hit, jnp.broadcast_to(whole[r : r + 1], (8, width)), acc)
        return acc

    lane, row8 = iota((8, 128), 1), iota((8, 128), 0)
    mine = by_slot(q_in)
    q_z[z] = jnp.concatenate([mine[0:4], mine[4:8]], axis=1)

    pl.semaphore_wait(barrier, len(peers))

    def qz_copy(d, origin):
        return remote(q_z.at[origin], q_z.at[origin], qz_s.at[d], qz_r.at[d], z_peer[0][d])

    qz = [qz_copy(d, z) for d in (4, 3, 5, 2, 6, 1, 7)]
    for c in qz:
        c.start()

    base = zq * 32 + y * 8
    for i, ref in enumerate((nk_in, nv_in)):
        part = by_slot(ref)
        acc = jnp.zeros((8, 128), F32)
        for f in range(8):
            acc = jnp.where(lane == base + f, jnp.broadcast_to(part[:, f : f + 1], (8, 128)), acc)
        new_y[0, 8 * i : 8 * i + 8] = acc
    new_y[0, 16:24] = jnp.where(lax.div(lane, 64) == half, jnp.concatenate([mine, mine], axis=1), 0.0)
    ny = [remote(new_y.at[0], new_y.at[d], ny_s.at[d], ny_r.at[d], xy_peer[0][d]) for d in range(1, NY)]
    for c in ny:
        c.start()

    slot_of = lax.rem(iota((64, CTX), 0), SLOTS)
    limit = jnp.zeros((64, CTX), I32)
    for s in range(SLOTS):
        n = jnp.int32(0)
        for r in range(8):
            n = n + jnp.where(slots[r] == core * SLOTS + s, len_ref[r], 0)
        limit = jnp.where(slot_of == s, n, limit)
    valid = seq * CTX + iota((64, CTX), 1) < limit
    slot_out = lax.rem(iota((64, HEAD_DIM), 0), SLOTS)
    left16, left32 = iota((16, 128), 1) < 64, iota((32, 128), 1) < 64

    for d in range(1, NZ):
        qz_copy(d, lax.rem(z + NZ - d, NZ)).wait_recv()
    q_xy[x, y] = jnp.concatenate([q_z[i] for i in range(NZ)], axis=0).astype(BF16)

    def qxy_copy(a, b, xx, yy):
        return remote(q_xy.at[xx, yy], q_xy.at[xx, yy], qxy_s.at[a, b], qxy_r.at[a, b], xy_peer[a][b])

    qxy = [qxy_copy(a, b, x, y) for a in (2, 1, 3, 0) for b in (2, 1, 3, 0) if a or b]
    for c in qxy:
        c.start()

    for c in ny:
        c.wait_recv()
    new_z[0] = (new_y[0, 0:16] + new_y[1, 0:16]) + (new_y[2, 0:16] + new_y[3, 0:16])
    nz = [remote(new_z.at[0], new_z.at[d], nz_s.at[d], nz_r.at[d], half_peer[d]) for d in range(1, 4)]
    for c in nz:
        c.start()

    for c in k_loads + v_loads:
        c.wait()

    def attend(xb, slot):
        turned = []
        for hh in range(2):
            a, b = q_xy[xb, 2 * hh].astype(F32), q_xy[xb, 2 * hh + 1].astype(F32)
            turned.append(jnp.where(left32, a, pltpu.roll(b, 64, 1)).astype(BF16))
            turned.append(jnp.where(left32, pltpu.roll(a, 64, 1), b).astype(BF16))
        ml = jnp.zeros((8, 128), F32)
        for j in range(2):
            cols = pl.ds(pl.multiple_of((xb * 2 + j) * HEAD_DIM, HEAD_DIM), HEAD_DIM)
            q = jnp.concatenate([u[16 * j : 16 * j + 16] for u in turned], axis=0)
            scores = None
            for s in range(SLOTS):
                part = lax.dot_general(q, k_buf[s, :, cols], (((1,), (1,)), ((), ())), preferred_element_type=F32)
                scores = part if s == 0 else jnp.where(slot_of == s, part, scores)
            scores = jnp.where(valid, scores * SCALE, NEG)
            top = jnp.max(scores, axis=1, keepdims=True)
            p = jnp.where(valid, jnp.exp2(scores - top), 0.0)
            total = jnp.sum(p, axis=1, keepdims=True)
            p = p.astype(BF16)
            out = None
            for s in range(SLOTS):
                part = jnp.dot(p, v_buf[s, :, cols], preferred_element_type=F32)
                out = part if s == 0 else jnp.where(slot_out == s, part, out)
            for hh in range(2):
                first, second = out[32 * hh : 32 * hh + 16], out[32 * hh + 16 : 32 * hh + 32]
                rows = slice(16 * j, 16 * j + 16)
                o_xy[slot, 2 * hh, rows] = jnp.where(left16, first, pltpu.roll(second, 64, 1)).astype(BF16)
                o_xy[slot, 2 * hh + 1, rows] = jnp.where(left16, pltpu.roll(first, 64, 1), second).astype(BF16)
                for t in range(2):
                    for rh in range(2):
                        here = slice(32 * hh + 16 * t + 8 * rh, 32 * hh + 16 * t + 8 * rh + 8)
                        i = hh * 8 + j * 4 + t * 2 + rh
                        ml = jnp.where(lane == i, top[here], ml)
                        ml = jnp.where(lane == 64 + i, total[here], ml)
        ml_xy[slot] = ml

    back = {}
    for a in range(NX):
        xb = lax.rem(x + NX - a, NX)
        for b in range(NY):
            if a or b:
                qxy_copy(a, b, xb, lax.rem(y + NY - b, NY)).wait_recv()
        attend(xb, a)
        for b in (2, 1, 3, 0):
            if a or b:
                target = xy_peer[(NX - a) % NX][b]
                yy = lax.rem(y + b, NY)
                back[a, b] = (
                    remote(o_xy.at[a, yy], o_in.at[a, b], o_s.at[a, b], o_r.at[a, b], target),
                    remote(ml_xy.at[a], ml_in.at[a, b], ml_s.at[a, b], ml_r.at[a, b], target),
                )
                for c in back[a, b]:
                    c.start()

    for c in nz:
        c.wait_recv()
    new = (new_z[0] + new_z[1]) + (new_z[2] + new_z[3])

    def spread(block):
        turned = jnp.concatenate([block[4:8], block[0:4]], axis=0)
        return jnp.where(row8 < 4, block, turned), jnp.where(row8 < 4, turned, block)

    key0, key1 = spread(new[0:8])
    val0, val1 = spread(new[8:16])
    qf = new_y[0, 16:24] + jnp.where(half == 0, new_y[3, 16:24], new_y[1, 16:24])
    second = iota((8, 1), 0) >= 4
    s0 = jnp.sum(qf * key0, axis=1, keepdims=True) * SCALE
    s1 = jnp.where(second, jnp.sum(qf * key1, axis=1, keepdims=True) * SCALE, NEG)
    new_top = jnp.maximum(s0, s1)
    p0 = jnp.exp2(s0 - new_top)
    p1 = jnp.where(second, jnp.exp2(s1 - new_top), 0.0)
    new_total = p0 + p1
    new_out = p0 * val0 + p1 * val1
    new_out = jnp.where(half == 0, new_out, pltpu.roll(new_out, 64, 1))

    for pairs in back.values():
        for c in pairs:
            c.wait_recv()
    mls = [ml_xy[0]] + [ml_in[a, b] for a, b in others]
    mls = [jnp.where(pair == 0, m, pltpu.roll(m, 120, 1)) for m in mls]
    outs = [o_xy.at[0, y]] + [o_in.at[a, b] for a, b in others]
    top = functools.reduce(jnp.maximum, mls)
    factors = [jnp.exp2(m - top) for m in mls]
    total = sum(pltpu.roll(f, 64, 1) * m for f, m in zip(factors, mls))
    for j in range(2):
        rows = [o[16 * j : 16 * j + 16].astype(F32) for o in outs]
        for rh in range(2):
            i = j * 4 + rh
            acc = sum(
                jnp.where(lane < 64, f[:, i : i + 1], f[:, i + 2 : i + 3]) * o[8 * rh : 8 * rh + 8]
                for f, o in zip(factors, rows)
            )
            swapped = pltpu.roll(acc, 64, 1)
            ends = [jnp.where(lane < 96, top[:, k : k + 1], total[:, 64 + k : 65 + k]) for k in (i, i + 2)]
            low = jnp.where(lane < 64, acc, ends[0])
            high = jnp.where(lane < 64, swapped, ends[1])
            zz = j * 4 + rh * 2
            fin[zz] = jnp.where(row8 < 4, low, pltpu.roll(high, 4, 0))
            fin[zz + 1] = jnp.where(row8 < 4, pltpu.roll(low, 4, 0), high)

    own = fin[z]
    best = jnp.maximum(own[:, 64:65], new_top)
    new_tile = jnp.where(lane < 64, new_out, new_total)
    own = jnp.exp2(own[:, 64:65] - best) * own + jnp.exp2(new_top - best) * new_tile
    fin[z] = jnp.where((lane >= 64) & (lane < 96), best, own)

    f = []
    for d in (4, 3, 5, 2, 6, 1, 7, 0):
        for other in range(2):
            if d or other:
                i = other * NZ + d
                f.append(remote(fin.at[lax.rem(z + d, NZ)], fin_in.at[i], f_s.at[i], f_r.at[i], z_peer[other][d]))
                f[-1].start()
    for c in f:
        c.wait_recv()

    parts = []
    for other in range(2):
        tiles = [fin_in[other * NZ + d] if d or other else fin[z] for d in range(NZ)]
        top = functools.reduce(jnp.maximum, tiles)
        acc = sum(jnp.exp2(t - top)[:, 64:65] * t for t in tiles)
        parts.append(acc[:, :64] / acc[:, 96:97])
    row = iota((8, 64), 0)
    slot_row = jnp.zeros((8, 64), I32)
    for r in range(8):
        slot_row = jnp.where(row == r, slots[r], slot_row)
    for t in range(2):
        result = jnp.zeros((8, 64), F32)
        for other in range(2):
            group = core + other - 2 * core * other
            for s in range(SLOTS):
                i = t * 4 + s
                found = slot_row == group * SLOTS + s
                result = jnp.where(found, jnp.broadcast_to(parts[other][i : i + 1], (8, 64)), result)
        out_ref[t] = result.astype(BF16)

    for c in ny + nz + qz + qxy + [c for pairs in back.values() for c in pairs] + f:
        c.wait_send()


def local(queries, new_keys, new_values, key_cache, value_cache, lengths, row_slot):
    sem = pltpu.SemaphoreType.DMA
    return pl.pallas_call(
        kernel,
        out_shape=jax.ShapeDtypeStruct(queries.shape, BF16),
        in_specs=[pl.BlockSpec(memory_space=pltpu.HBM)] * 7,
        out_specs=pl.BlockSpec(memory_space=pltpu.VMEM),
        scratch_shapes=[
            pltpu.VMEM(queries.shape, BF16),
            pltpu.VMEM(new_keys.shape, BF16),
            pltpu.VMEM(new_values.shape, BF16),
            pltpu.SMEM(lengths.shape, I32),
            pltpu.SMEM(row_slot.shape, I32),
            pltpu.VMEM(key_cache.shape, BF16),
            pltpu.VMEM(value_cache.shape, BF16),
            pltpu.VMEM((NY, 24, 128), F32),
            pltpu.VMEM((4, 16, 128), F32),
            pltpu.VMEM((NZ, 4, 128), F32),
            pltpu.VMEM((NX, NY, 32, 128), BF16),
            pltpu.VMEM((NX, NY, 32, 128), BF16),
            pltpu.VMEM((NX, 8, 128), F32),
            pltpu.VMEM((NX, NY, 32, 128), BF16),
            pltpu.VMEM((NX, NY, 8, 128), F32),
            pltpu.VMEM((NZ, 8, 128), F32),
            pltpu.VMEM((2 * NZ, 8, 128), F32),
            sem((5,)), sem((2 * SLOTS,)),
            sem((NY,)), sem((NY,)), sem((4,)), sem((4,)), sem((NZ,)), sem((NZ,)),
            sem((NX, NY)), sem((NX, NY)), sem((NX, NY)), sem((NX, NY)), sem((NX, NY)), sem((NX, NY)),
            sem((2 * NZ,)), sem((2 * NZ,)),
        ],
        compiler_params=pltpu.CompilerParams(
            collective_id=0, has_side_effects=True, vmem_limit_bytes=64 * 1024 * 1024
        ),
    )(queries, new_keys, new_values, key_cache, value_cache, lengths, row_slot)


def solution(mesh):
    in_specs = (
        P(None, None, "seq"),
        P(None, None, "seq"),
        P(None, None, "seq"),
        P("rows", "seq", None),
        P("rows", "seq", None),
        P(),
        P(),
    )
    out_specs = P(None, None, "seq")
    return jax.shard_map(local, mesh=mesh, in_specs=in_specs, out_specs=out_specs, check_vma=False)
```

time: 39.9 us -> 35.8 us (0.90)
  Pallas kernels: 38.5 us -> 34.3 us
    pallas_call x1, Pallas kernels: 38.5 us -> 34.3 us  [local(): pl.pallas_call(kernel, out_shape=jax.ShapeDtypeStruct(queries.shape, BF16...]
where the time goes in v3:
time: 35.8 us; the launch traced here: 35.6 us
  Pallas kernels  34.3 us (96%)
  local copies, waits for them, and re-layouts  1.28 us (4%)
    pallas_call x1, Pallas kernels, local(): pl.pallas_call(kernel, out_shape=jax.ShapeDtypeStruct(queries.shape, BF16...  34.3 us
    unnamed x1, local copies, waits for them, and re-layouts  1.28 us

profile of v3, /device:TPU:1, one launch (start us, length us, event | category | flops | bytes accessed | tf_op | source)
XLA Modules:
  0.0 35.6 jit_solution(9851223827483649777)
XLA Ops:
  0.0 34.3 %shard_map.73 = bf16[2,8,64]{2,1,0:T(8,128)(2,1)} custom-call(bf16[2,8,64]{2,1,0:T(8,128)(2,1)} %q_hbm.1, bf16[2,8,8]{2,1,0:T(8,128)(2,1)} %nk_hbm.1, bf16[2,8,8]{2,1,0:T(8,128)(2,1)} %nv_hbm.1, bf16[4,256,1024]{2,1,0:T(8,128)(2,1)} %k_hbm.1, bf16[4,256,1024]{2,1,0:T(8,128)(2,1)} %v_hbm.1, s32[8]{0:T(128)} %len_hbm.1, s32[8]{0:T(128)} %slot_hbm.1), custom_call_target="tpu_custom_call" | custom-call | tf_op jit(solution)/shard_map/pallas_call | solution.py:285
  34.3 1.3 %copy.9 = bf16[2,8,64]{2,1,0:T(8,128)(2,1)} copy(bf16[2,8,64]{2,1,0:T(8,128)(2,1)} %shard_map.73) | data formatting | bytes 4096

commit v4 on v3

--- a/solution.py
+++ b/solution.py
@@ -282,6 +282,7 @@
 
 def local(queries, new_keys, new_values, key_cache, value_cache, lengths, row_slot):
     sem = pltpu.SemaphoreType.DMA
+    args = (queries, new_keys, new_values, key_cache, value_cache, lengths, row_slot)
     return pl.pallas_call(
         kernel,
         out_shape=jax.ShapeDtypeStruct(queries.shape, BF16),
@@ -311,9 +312,9 @@
             sem((2 * NZ,)), sem((2 * NZ,)),
         ],
         compiler_params=pltpu.CompilerParams(
-            collective_id=0, has_side_effects=True, vmem_limit_bytes=64 * 1024 * 1024
+            collective_id=0, has_side_effects=True, vmem_limit_bytes=48 * 1024 * 1024
         ),
-    )(queries, new_keys, new_values, key_cache, value_cache, lengths, row_slot)
+    )(*(pltpu.with_memory_space_constraint(a, pltpu.HBM) for a in args))
 
 
 def solution(mesh):

time: 35.8 us -> 34.4 us (0.961)
  local copies, waits for them, and re-layouts: 1.28 us -> 0.6 us
  Pallas kernels: 34.3 us -> 33.7 us
    unnamed x1, local copies, waits for them, and re-layouts: 1.28 us -> 0.6 us
    pallas_call x1, Pallas kernels: 34.3 us -> 33.7 us  [local(): pl.pallas_call(kernel, out_shape=jax.ShapeDtypeStruct(queries.shape, BF16...]
where the time goes in v4:
time: 34.4 us; the launch traced here: 34.3 us
  Pallas kernels  33.7 us (98%)
  local copies, waits for them, and re-layouts  0.6 us (2%)
    pallas_call x1, Pallas kernels, local(): pl.pallas_call(kernel, out_shape=jax.ShapeDtypeStruct(queries.shape, BF16...  33.7 us

profile of v4, /device:TPU:1, one launch (start us, length us, event | category | flops | bytes accessed | tf_op | source)
XLA Modules:
  0.0 34.3 jit_solution(7625353379049613244)
XLA Ops:
  0.0 33.7 %shard_map.73 = bf16[2,8,64]{2,1,0:T(8,128)(2,1)S(1)} custom-call(bf16[2,8,64]{2,1,0:T(8,128)(2,1)} %q_hbm.1, bf16[2,8,8]{2,1,0:T(8,128)(2,1)} %nk_hbm.1, bf16[2,8,8]{2,1,0:T(8,128)(2,1)} %nv_hbm.1, bf16[4,256,1024]{2,1,0:T(8,128)(2,1)} %k_hbm.1, bf16[4,256,1024]{2,1,0:T(8,128)(2,1)} %v_hbm.1, s32[8]{0:T(128)} %len_hbm.1, s32[8]{0:T(128)} %slot_hbm.1), custom_call_target="tpu_custom_call" | custom-call | tf_op jit(solution)/shard_map/pallas_call | solution.py:286
  33.7 0.6 %copy.9 = bf16[2,8,64]{2,1,0:T(8,128)(2,1)} copy(bf16[2,8,64]{2,1,0:T(8,128)(2,1)S(1)} %shard_map.73) | data formatting | bytes 4096

commit v5 on v4

--- a/solution.py
+++ b/solution.py
@@ -24,9 +24,9 @@
 def kernel(
     q_hbm, nk_hbm, nv_hbm, k_hbm, v_hbm, len_hbm, slot_hbm, out_ref,
     q_in, nk_in, nv_in, len_ref, slot_ref, k_buf, v_buf,
-    new_y, new_z, q_z, q_xy, o_xy, ml_xy, o_in, ml_in, fin, fin_in,
+    new_y, new_z, new_tile, q_z, q_xy, o_xy, ml_xy, o_in, ml_in, fin, fin_in,
     in_sem, cache_sem,
-    ny_s, ny_r, nz_s, nz_r, qz_s, qz_r, qxy_s, qxy_r, o_s, o_r, ml_s, ml_r, f_s, f_r,
+    ny_s, ny_r, nz_s, nz_r, nc_s, nc_r, qz_s, qz_r, qxy_s, qxy_r, o_s, o_r, ml_s, ml_r, f_s, f_r,
 ):
     seq, core = lax.axis_index("seq"), lax.axis_index("rows")
     y = lax.rem(seq, NY)
@@ -108,15 +108,14 @@
     for c in ny:
         c.start()
 
-    slot_of = lax.rem(iota((64, CTX), 0), SLOTS)
-    limit = jnp.zeros((64, CTX), I32)
+    slot_of = lax.rem(iota((128, CTX), 0), SLOTS)
+    limit = jnp.zeros((128, CTX), I32)
     for s in range(SLOTS):
         n = jnp.int32(0)
         for r in range(8):
             n = n + jnp.where(slots[r] == core * SLOTS + s, len_ref[r], 0)
         limit = jnp.where(slot_of == s, n, limit)
-    valid = seq * CTX + iota((64, CTX), 1) < limit
-    slot_out = lax.rem(iota((64, HEAD_DIM), 0), SLOTS)
+    valid = seq * CTX + iota((128, CTX), 1) < limit
     left16, left32 = iota((16, 128), 1) < 64, iota((32, 128), 1) < 64
 
     for d in range(1, NZ):
@@ -146,23 +145,28 @@
             a, b = q_xy[xb, 2 * hh].astype(F32), q_xy[xb, 2 * hh + 1].astype(F32)
             turned.append(jnp.where(left32, a, pltpu.roll(b, 64, 1)).astype(BF16))
             turned.append(jnp.where(left32, pltpu.roll(a, 64, 1), b).astype(BF16))
+        cols = pl.ds(pl.multiple_of(xb * 2 * HEAD_DIM, 2 * HEAD_DIM), 2 * HEAD_DIM)
+        none = jnp.zeros((64, HEAD_DIM), BF16)
+        q0, q1 = (jnp.concatenate([u[16 * j : 16 * j + 16] for u in turned], axis=0) for j in range(2))
+        q = jnp.concatenate(
+            [jnp.concatenate([q0, none], axis=1), jnp.concatenate([none, q1], axis=1)], axis=0
+        )
+        scores = None
+        for s in range(SLOTS):
+            part = lax.dot_general(q, k_buf[s, :, cols], (((1,), (1,)), ((), ())), preferred_element_type=F32)
+            scores = part if s == 0 else jnp.where(slot_of == s, part, scores)
+        scores = jnp.where(valid, scores * SCALE, NEG)
+        top = jnp.maximum(jnp.max(scores, axis=1, keepdims=True), NEG / 2)
+        p = jnp.exp2(scores - top)
+        total = jnp.sum(p, axis=1, keepdims=True)
+        p = p.astype(BF16)
+        sums = None
+        for s in range(SLOTS):
+            part = jnp.dot(p, v_buf[s, :, cols], preferred_element_type=F32)
+            sums = part if s == 0 else jnp.where(slot_of == s, part, sums)
         ml = jnp.zeros((8, 128), F32)
         for j in range(2):
-            cols = pl.ds(pl.multiple_of((xb * 2 + j) * HEAD_DIM, HEAD_DIM), HEAD_DIM)
-            q = jnp.concatenate([u[16 * j : 16 * j + 16] for u in turned], axis=0)
-            scores = None
-            for s in range(SLOTS):
-                part = lax.dot_general(q, k_buf[s, :, cols], (((1,), (1,)), ((), ())), preferred_element_type=F32)
-                scores = part if s == 0 else jnp.where(slot_of == s, part, scores)
-            scores = jnp.where(valid, scores * SCALE, NEG)
-            top = jnp.max(scores, axis=1, keepdims=True)
-            p = jnp.where(valid, jnp.exp2(scores - top), 0.0)
-            total = jnp.sum(p, axis=1, keepdims=True)
-            p = p.astype(BF16)
-            out = None
-            for s in range(SLOTS):
-                part = jnp.dot(p, v_buf[s, :, cols], preferred_element_type=F32)
-                out = part if s == 0 else jnp.where(slot_out == s, part, out)
+            out = sums[64 * j : 64 * j + 64, HEAD_DIM * j : HEAD_DIM * j + HEAD_DIM]
             for hh in range(2):
                 first, second = out[32 * hh : 32 * hh + 16], out[32 * hh + 16 : 32 * hh + 32]
                 rows = slice(16 * j, 16 * j + 16)
@@ -170,7 +174,8 @@
                 o_xy[slot, 2 * hh + 1, rows] = jnp.where(left16, pltpu.roll(first, 64, 1), second).astype(BF16)
                 for t in range(2):
                     for rh in range(2):
-                        here = slice(32 * hh + 16 * t + 8 * rh, 32 * hh + 16 * t + 8 * rh + 8)
+                        start = 64 * j + 32 * hh + 16 * t + 8 * rh
+                        here = slice(start, start + 8)
                         i = hh * 8 + j * 4 + t * 2 + rh
                         ml = jnp.where(lane == i, top[here], ml)
                         ml = jnp.where(lane == 64 + i, total[here], ml)
@@ -214,6 +219,9 @@
     new_total = p0 + p1
     new_out = p0 * val0 + p1 * val1
     new_out = jnp.where(half == 0, new_out, pltpu.roll(new_out, 64, 1))
+    new_tile[0] = jnp.where(lane < 64, new_out, jnp.where(lane < 96, new_top, new_total))
+    nc = remote(new_tile.at[0], new_tile.at[1], nc_s, nc_r, z_peer[1][0])
+    nc.start()
 
     for pairs in back.values():
         for c in pairs:
@@ -240,12 +248,6 @@
             fin[zz] = jnp.where(row8 < 4, low, pltpu.roll(high, 4, 0))
             fin[zz + 1] = jnp.where(row8 < 4, pltpu.roll(low, 4, 0), high)
 
-    own = fin[z]
-    best = jnp.maximum(own[:, 64:65], new_top)
-    new_tile = jnp.where(lane < 64, new_out, new_total)
-    own = jnp.exp2(own[:, 64:65] - best) * own + jnp.exp2(new_top - best) * new_tile
-    fin[z] = jnp.where((lane >= 64) & (lane < 96), best, own)
-
     f = []
     for d in (4, 3, 5, 2, 6, 1, 7, 0):
         for other in range(2):
@@ -253,12 +255,12 @@
                 i = other * NZ + d
                 f.append(remote(fin.at[lax.rem(z + d, NZ)], fin_in.at[i], f_s.at[i], f_r.at[i], z_peer[other][d]))
                 f[-1].start()
-    for c in f:
+    for c in [nc] + f:
         c.wait_recv()
 
     parts = []
     for other in range(2):
-        tiles = [fin_in[other * NZ + d] if d or other else fin[z] for d in range(NZ)]
+        tiles = [fin_in[other * NZ + d] if d or other else fin[z] for d in range(NZ)] + [new_tile[other]]
         top = functools.reduce(jnp.maximum, tiles)
         acc = sum(jnp.exp2(t - top)[:, 64:65] * t for t in tiles)
         parts.append(acc[:, :64] / acc[:, 96:97])
@@ -276,7 +278,7 @@
                 result = jnp.where(found, jnp.broadcast_to(parts[other][i : i + 1], (8, 64)), result)
         out_ref[t] = result.astype(BF16)
 
-    for c in ny + nz + qz + qxy + [c for pairs in back.values() for c in pairs] + f:
+    for c in [nc] + ny + nz + qz + qxy + [c for pairs in back.values() for c in pairs] + f:
         c.wait_send()
 
 
@@ -298,6 +300,7 @@
             pltpu.VMEM(value_cache.shape, BF16),
             pltpu.VMEM((NY, 24, 128), F32),
             pltpu.VMEM((4, 16, 128), F32),
+            pltpu.VMEM((2, 8, 128), F32),
             pltpu.VMEM((NZ, 4, 128), F32),
             pltpu.VMEM((NX, NY, 32, 128), BF16),
             pltpu.VMEM((NX, NY, 32, 128), BF16),
@@ -307,7 +310,7 @@
             pltpu.VMEM((NZ, 8, 128), F32),
             pltpu.VMEM((2 * NZ, 8, 128), F32),
             sem((5,)), sem((2 * SLOTS,)),
-            sem((NY,)), sem((NY,)), sem((4,)), sem((4,)), sem((NZ,)), sem((NZ,)),
+            sem((NY,)), sem((NY,)), sem((4,)), sem((4,)), sem, sem, sem((NZ,)), sem((NZ,)),
             sem((NX, NY)), sem((NX, NY)), sem((NX, NY)), sem((NX, NY)), sem((NX, NY)), sem((NX, NY)),
             sem((2 * NZ,)), sem((2 * NZ,)),
         ],

time: 34.4 us -> 33.5 us (0.974)
  Pallas kernels: 33.7 us -> 32.8 us
    pallas_call x1, Pallas kernels: 33.7 us -> 32.8 us  [local(): pl.pallas_call(kernel, out_shape=jax.ShapeDtypeStruct(queries.shape, BF16...]
where the time goes in v5:
time: 33.5 us; the launch traced here: 33.4 us
  Pallas kernels  32.8 us (98%)
  local copies, waits for them, and re-layouts  0.6 us (2%)
    pallas_call x1, Pallas kernels, local(): pl.pallas_call(kernel, out_shape=jax.ShapeDtypeStruct(queries.shape, BF16...  32.8 us

profile of v5, /device:TPU:1, one launch (start us, length us, event | category | flops | bytes accessed | tf_op | source)
XLA Modules:
  0.0 33.4 jit_solution(1551544576230793137)
XLA Ops:
  0.0 32.8 %shard_map.73 = bf16[2,8,64]{2,1,0:T(8,128)(2,1)S(1)} custom-call(bf16[2,8,64]{2,1,0:T(8,128)(2,1)} %q_hbm.1, bf16[2,8,8]{2,1,0:T(8,128)(2,1)} %nk_hbm.1, bf16[2,8,8]{2,1,0:T(8,128)(2,1)} %nv_hbm.1, bf16[4,256,1024]{2,1,0:T(8,128)(2,1)} %k_hbm.1, bf16[4,256,1024]{2,1,0:T(8,128)(2,1)} %v_hbm.1, s32[8]{0:T(128)} %len_hbm.1, s32[8]{0:T(128)} %slot_hbm.1), custom_call_target="tpu_custom_call" | custom-call | tf_op jit(solution)/shard_map/pallas_call | solution.py:288
  32.8 0.6 %copy.9 = bf16[2,8,64]{2,1,0:T(8,128)(2,1)} copy(bf16[2,8,64]{2,1,0:T(8,128)(2,1)S(1)} %shard_map.73) | data formatting | bytes 4096

commit v6 on v5

--- a/solution.py
+++ b/solution.py
@@ -48,6 +48,12 @@
     half_peer = [at(x, z - zq + lax.rem(zq + d, 4), y, core) for d in range(4)]
     others = [(a, b) for a in range(NX) for b in range(NY) if a or b]
 
+    barrier = pltpu.get_barrier_semaphore()
+    far = (4, 3, 5, 2, 6, 1, 7)
+    peers = [z_peer[i][d] for d in far for i in (1, 0)] + [xy_peer[a][b] for a in (2, 1, 3, 0) for b in (2, 1, 3, 0) if a or b] + [z_peer[1][0]]
+    for p in peers:
+        pl.semaphore_signal(barrier, inc=1, device_id=p, device_id_type=MESH)
+
     loads = [
         pltpu.make_async_copy(q_hbm, q_in, in_sem.at[0]),
         pltpu.make_async_copy(slot_hbm, slot_ref, in_sem.at[1]),
@@ -57,11 +63,6 @@
     ]
     for c in loads:
         c.start()
-
-    barrier = pltpu.get_barrier_semaphore()
-    peers = z_peer[0][1:] + z_peer[1] + [xy_peer[a][b] for a, b in others]
-    for p in peers:
-        pl.semaphore_signal(barrier, inc=1, device_id=p, device_id_type=MESH)
 
     k_loads = [pltpu.make_async_copy(k_hbm.at[s], k_buf.at[s], cache_sem.at[s]) for s in range(SLOTS)]
     v_loads = [pltpu.make_async_copy(v_hbm.at[s], v_buf.at[s], cache_sem.at[SLOTS + s]) for s in range(SLOTS)]
@@ -193,8 +194,8 @@
                 target = xy_peer[(NX - a) % NX][b]
                 yy = lax.rem(y + b, NY)
                 back[a, b] = (
+                    remote(ml_xy.at[a], ml_in.at[a, b], ml_s.at[a, b], ml_r.at[a, b], target),
                     remote(o_xy.at[a, yy], o_in.at[a, b], o_s.at[a, b], o_r.at[a, b], target),
-                    remote(ml_xy.at[a], ml_in.at[a, b], ml_s.at[a, b], ml_r.at[a, b], target),
                 )
                 for c in back[a, b]:
                     c.start()
@@ -223,23 +224,36 @@
     nc = remote(new_tile.at[0], new_tile.at[1], nc_s, nc_r, z_peer[1][0])
     nc.start()
 
-    for pairs in back.values():
-        for c in pairs:
-            c.wait_recv()
-    mls = [ml_xy[0]] + [ml_in[a, b] for a, b in others]
-    mls = [jnp.where(pair == 0, m, pltpu.roll(m, 120, 1)) for m in mls]
-    outs = [o_xy.at[0, y]] + [o_in.at[a, b] for a, b in others]
-    top = functools.reduce(jnp.maximum, mls)
-    factors = [jnp.exp2(m - top) for m in mls]
-    total = sum(pltpu.roll(f, 64, 1) * m for f, m in zip(factors, mls))
+    def by_lane(tile, i):
+        return jnp.where(lane < 64, tile[:, i : i + 1], tile[:, i + 2 : i + 3])
+
+    def gathered(group):
+        keys = [(a, b) for a in group for b in range(NY)]
+        for i in range(2):
+            for key in keys:
+                if key in back:
+                    back[key][i].wait_recv()
+        mls = [ml_in[a, b] if a or b else ml_xy[0] for a, b in keys]
+        mls = [jnp.where(pair == 0, m, pltpu.roll(m, 120, 1)) for m in mls]
+        outs = [o_in.at[a, b] if a or b else o_xy.at[0, y] for a, b in keys]
+        top = functools.reduce(jnp.maximum, mls)
+        factors = [jnp.exp2(m - top) for m in mls]
+        total = sum(pltpu.roll(f, 64, 1) * m for f, m in zip(factors, mls))
+        sums = []
+        for j in range(2):
+            rows = [o[16 * j : 16 * j + 16].astype(F32) for o in outs]
+            for rh in range(2):
+                sums.append(sum(by_lane(f, j * 4 + rh) * o[8 * rh : 8 * rh + 8] for f, o in zip(factors, rows)))
+        return top, total, sums
+
+    early, late = gathered((0, 1)), gathered((2, 3))
+    top = jnp.maximum(early[0], late[0])
+    factors = [jnp.exp2(g[0] - top) for g in (early, late)]
+    total = sum(pltpu.roll(f, 64, 1) * g[1] for f, g in zip(factors, (early, late)))
     for j in range(2):
-        rows = [o[16 * j : 16 * j + 16].astype(F32) for o in outs]
         for rh in range(2):
             i = j * 4 + rh
-            acc = sum(
-                jnp.where(lane < 64, f[:, i : i + 1], f[:, i + 2 : i + 3]) * o[8 * rh : 8 * rh + 8]
-                for f, o in zip(factors, rows)
-            )
+            acc = sum(by_lane(f, i) * g[2][2 * j + rh] for f, g in zip(factors, (early, late)))
             swapped = pltpu.roll(acc, 64, 1)
             ends = [jnp.where(lane < 96, top[:, k : k + 1], total[:, 64 + k : 65 + k]) for k in (i, i + 2)]
             low = jnp.where(lane < 64, acc, ends[0])
@@ -255,6 +269,12 @@
                 i = other * NZ + d
                 f.append(remote(fin.at[lax.rem(z + d, NZ)], fin_in.at[i], f_s.at[i], f_r.at[i], z_peer[other][d]))
                 f[-1].start()
+    row = iota((8, 64), 0)
+    slot_row = jnp.zeros((8, 64), I32)
+    for r in range(8):
+        slot_row = jnp.where(row == r, slots[r], slot_row)
+    for c in [nc] + ny + nz + qz + qxy + [c for pairs in back.values() for c in pairs]:
+        c.wait_send()
     for c in [nc] + f:
         c.wait_recv()
 
@@ -264,10 +284,6 @@
         top = functools.reduce(jnp.maximum, tiles)
         acc = sum(jnp.exp2(t - top)[:, 64:65] * t for t in tiles)
         parts.append(acc[:, :64] / acc[:, 96:97])
-    row = iota((8, 64), 0)
-    slot_row = jnp.zeros((8, 64), I32)
-    for r in range(8):
-        slot_row = jnp.where(row == r, slots[r], slot_row)
     for t in range(2):
         result = jnp.zeros((8, 64), F32)
         for other in range(2):
@@ -278,7 +294,7 @@
                 result = jnp.where(found, jnp.broadcast_to(parts[other][i : i + 1], (8, 64)), result)
         out_ref[t] = result.astype(BF16)
 
-    for c in [nc] + ny + nz + qz + qxy + [c for pairs in back.values() for c in pairs] + f:
+    for c in f:
         c.wait_send()
 
 

time: 33.5 us -> 33.3 us (level)
  no operation moved by 1% of the time
where the time goes in v6:
time: 33.3 us; the launch traced here: 33.2 us
  Pallas kernels  32.6 us (98%)
  local copies, waits for them, and re-layouts  0.6 us (2%)
    pallas_call x1, Pallas kernels, local(): pl.pallas_call(kernel, out_shape=jax.ShapeDtypeStruct(queries.shape, BF16...  32.6 us

profile of v6, /device:TPU:1, one launch (start us, length us, event | category | flops | bytes accessed | tf_op | source)
XLA Modules:
  0.0 33.2 jit_solution(6483211627674944854)
XLA Ops:
  0.0 32.6 %shard_map.73 = bf16[2,8,64]{2,1,0:T(8,128)(2,1)S(1)} custom-call(bf16[2,8,64]{2,1,0:T(8,128)(2,1)} %q_hbm.1, bf16[2,8,8]{2,1,0:T(8,128)(2,1)} %nk_hbm.1, bf16[2,8,8]{2,1,0:T(8,128)(2,1)} %nv_hbm.1, bf16[4,256,1024]{2,1,0:T(8,128)(2,1)} %k_hbm.1, bf16[4,256,1024]{2,1,0:T(8,128)(2,1)} %v_hbm.1, s32[8]{0:T(128)} %len_hbm.1, s32[8]{0:T(128)} %slot_hbm.1), custom_call_target="tpu_custom_call" | custom-call | tf_op jit(solution)/shard_map/pallas_call | solution.py:304
  32.6 0.6 %copy.9 = bf16[2,8,64]{2,1,0:T(8,128)(2,1)} copy(bf16[2,8,64]{2,1,0:T(8,128)(2,1)S(1)} %shard_map.73) | data formatting | bytes 4096

commit v7 on v6

--- a/solution.py
+++ b/solution.py
@@ -66,8 +66,6 @@
 
     k_loads = [pltpu.make_async_copy(k_hbm.at[s], k_buf.at[s], cache_sem.at[s]) for s in range(SLOTS)]
     v_loads = [pltpu.make_async_copy(v_hbm.at[s], v_buf.at[s], cache_sem.at[SLOTS + s]) for s in range(SLOTS)]
-    for c in k_loads + v_loads:
-        c.start()
     for c in loads:
         c.wait()
     slots = [slot_ref[r] for r in range(8)]
@@ -94,7 +92,7 @@
         return remote(q_z.at[origin], q_z.at[origin], qz_s.at[d], qz_r.at[d], z_peer[0][d])
 
     qz = [qz_copy(d, z) for d in (4, 3, 5, 2, 6, 1, 7)]
-    for c in qz:
+    for c in qz + k_loads + v_loads:
         c.start()
 
     base = zq * 32 + y * 8
@@ -264,7 +262,7 @@
 
     f = []
     for d in (4, 3, 5, 2, 6, 1, 7, 0):
-        for other in range(2):
+        for other in (1, 0):
             if d or other:
                 i = other * NZ + d
                 f.append(remote(fin.at[lax.rem(z + d, NZ)], fin_in.at[i], f_s.at[i], f_r.at[i], z_peer[other][d]))

time: 33.3 us -> 33.1 us (level)
  no operation moved by 1% of the time
where the time goes in v7:
time: 33.1 us; the launch traced here: 32.9 us
  Pallas kernels  32.3 us (98%)
  local copies, waits for them, and re-layouts  0.6 us (2%)
    pallas_call x1, Pallas kernels, local(): pl.pallas_call(kernel, out_shape=jax.ShapeDtypeStruct(queries.shape, BF16...  32.3 us

profile of v7, /device:TPU:1, one launch (start us, length us, event | category | flops | bytes accessed | tf_op | source)
XLA Modules:
  0.0 32.9 jit_solution(8942995762653110857)
XLA Ops:
  0.0 32.3 %shard_map.73 = bf16[2,8,64]{2,1,0:T(8,128)(2,1)S(1)} custom-call(bf16[2,8,64]{2,1,0:T(8,128)(2,1)} %q_hbm.1, bf16[2,8,8]{2,1,0:T(8,128)(2,1)} %nk_hbm.1, bf16[2,8,8]{2,1,0:T(8,128)(2,1)} %nv_hbm.1, bf16[4,256,1024]{2,1,0:T(8,128)(2,1)} %k_hbm.1, bf16[4,256,1024]{2,1,0:T(8,128)(2,1)} %v_hbm.1, s32[8]{0:T(128)} %len_hbm.1, s32[8]{0:T(128)} %slot_hbm.1), custom_call_target="tpu_custom_call" | custom-call | tf_op jit(solution)/shard_map/pallas_call | solution.py:302
  32.4 0.6 %copy.9 = bf16[2,8,64]{2,1,0:T(8,128)(2,1)} copy(bf16[2,8,64]{2,1,0:T(8,128)(2,1)S(1)} %shard_map.73) | data formatting | bytes 4096

commit v8 on v7

--- a/solution.py
+++ b/solution.py
@@ -163,7 +163,7 @@
         for s in range(SLOTS):
             part = jnp.dot(p, v_buf[s, :, cols], preferred_element_type=F32)
             sums = part if s == 0 else jnp.where(slot_of == s, part, sums)
-        ml = jnp.zeros((8, 128), F32)
+        ml = [jnp.zeros((8, 128), F32)] * 2
         for j in range(2):
             out = sums[64 * j : 64 * j + 64, HEAD_DIM * j : HEAD_DIM * j + HEAD_DIM]
             for hh in range(2):
@@ -175,10 +175,10 @@
                     for rh in range(2):
                         start = 64 * j + 32 * hh + 16 * t + 8 * rh
                         here = slice(start, start + 8)
-                        i = hh * 8 + j * 4 + t * 2 + rh
-                        ml = jnp.where(lane == i, top[here], ml)
-                        ml = jnp.where(lane == 64 + i, total[here], ml)
-        ml_xy[slot] = ml
+                        i = j * 4 + t * 2 + rh
+                        ml[hh] = jnp.where(lane == i, top[here], ml[hh])
+                        ml[hh] = jnp.where(lane == 64 + i, total[here], ml[hh])
+        ml_xy[slot, 0], ml_xy[slot, 1] = ml
 
     back = {}
     for a in range(NX):
@@ -192,7 +192,7 @@
                 target = xy_peer[(NX - a) % NX][b]
                 yy = lax.rem(y + b, NY)
                 back[a, b] = (
-                    remote(ml_xy.at[a], ml_in.at[a, b], ml_s.at[a, b], ml_r.at[a, b], target),
+                    remote(ml_xy.at[a, lax.div(yy, 2)], ml_in.at[a, b], ml_s.at[a, b], ml_r.at[a, b], target),
                     remote(o_xy.at[a, yy], o_in.at[a, b], o_s.at[a, b], o_r.at[a, b], target),
                 )
                 for c in back[a, b]:
@@ -231,8 +231,7 @@
             for key in keys:
                 if key in back:
                     back[key][i].wait_recv()
-        mls = [ml_in[a, b] if a or b else ml_xy[0] for a, b in keys]
-        mls = [jnp.where(pair == 0, m, pltpu.roll(m, 120, 1)) for m in mls]
+        mls = [ml_in[a, b] if a or b else ml_xy[0, pair] for a, b in keys]
         outs = [o_in.at[a, b] if a or b else o_xy.at[0, y] for a, b in keys]
         top = functools.reduce(jnp.maximum, mls)
         factors = [jnp.exp2(m - top) for m in mls]
@@ -318,7 +317,7 @@
             pltpu.VMEM((NZ, 4, 128), F32),
             pltpu.VMEM((NX, NY, 32, 128), BF16),
             pltpu.VMEM((NX, NY, 32, 128), BF16),
-            pltpu.VMEM((NX, 8, 128), F32),
+            pltpu.VMEM((NX, 2, 8, 128), F32),
             pltpu.VMEM((NX, NY, 32, 128), BF16),
             pltpu.VMEM((NX, NY, 8, 128), F32),
             pltpu.VMEM((NZ, 8, 128), F32),

time: 33.1 us -> 33 us (level)
  no operation moved by 1% of the time
where the time goes in v8:
time: 33 us; the launch traced here: 32.9 us
  Pallas kernels  32.3 us (98%)
  local copies, waits for them, and re-layouts  0.6 us (2%)
    pallas_call x1, Pallas kernels, local(): pl.pallas_call(kernel, out_shape=jax.ShapeDtypeStruct(queries.shape, BF16...  32.3 us

profile of v8, /device:TPU:1, one launch (start us, length us, event | category | flops | bytes accessed | tf_op | source)
XLA Modules:
  0.0 32.9 jit_solution(12687580328278281527)
XLA Ops:
  0.0 32.3 %shard_map.73 = bf16[2,8,64]{2,1,0:T(8,128)(2,1)S(1)} custom-call(bf16[2,8,64]{2,1,0:T(8,128)(2,1)} %q_hbm.1, bf16[2,8,8]{2,1,0:T(8,128)(2,1)} %nk_hbm.1, bf16[2,8,8]{2,1,0:T(8,128)(2,1)} %nv_hbm.1, bf16[4,256,1024]{2,1,0:T(8,128)(2,1)} %k_hbm.1, bf16[4,256,1024]{2,1,0:T(8,128)(2,1)} %v_hbm.1, s32[8]{0:T(128)} %len_hbm.1, s32[8]{0:T(128)} %slot_hbm.1), custom_call_target="tpu_custom_call" | custom-call | tf_op jit(solution)/shard_map/pallas_call | solution.py:301
  32.3 0.6 %copy.9 = bf16[2,8,64]{2,1,0:T(8,128)(2,1)} copy(bf16[2,8,64]{2,1,0:T(8,128)(2,1)S(1)} %shard_map.73) | data formatting | bytes 4096
